TPU v7x, 256 devices: a whole 4x4x8 slice. The times are simulated.
256 devices in a mesh: dp: 2 (over x_lo), seq: 16 (over z, core), fsdp: 8 (over x_hi, y).
Axes of the slice: x: 4 (x_hi: 2, x_lo: 2; x = x_hi * 2 + x_lo), y: 4, z: 8, core: 2. Of those that a mesh axis runs over, the one named last changes fastest.
Arguments:
- queries_raw: bfloat16 [16, 4096, 2048], P(('dp', 'fsdp'), 'seq'), parts along dimension 0, may hold values from -6 to 6
- keys_values: bfloat16 [16, 4096, 2048], P(('dp', 'fsdp'), 'seq'), parts along dimension 0, may hold values from -6 to 6
- doc_ids: int32 [16, 4096], P(('dp', 'fsdp')), parts along dimension 0, may hold values from 0 to 3, never falling along the last dimension, each value on 1 to 2048 neighbouring positions
- q_gain: float32 [128], replicated, may hold values from 0.6 to 7
- k_gain: float32 [128], replicated, may hold values from 0.6 to 7
- out_weight: bfloat16 [2048, 5376], P('fsdp'), may hold values from -0.125 to 0.125
- post_gain: float32 [5376], replicated, may hold values from 0.25 to 1.75
Outputs:
- layer_out: bfloat16 [16, 4096, 5376], P(('dp', 'fsdp'), 'seq'), parts along dimension 0
There are 2 independent parts, one for each index of `dp`. A program takes and returns all parts, laid end to end along the dimension named above; an argument that names none is the same for every part. Nothing has to cross between parts.
Inputs may be any that keep to these rules, and one draw needn't show every extreme that they name: `doc_ids`: each slab's document numbers never fall; a document has at most 2048 tokens, and one has exactly that many.
All inputs are finite; a program needn't handle non-finite values.
Results may differ from a plain program's by a relative error of at most 0.008.
The roundings to bfloat16 on the way count: a program that leaves them out, or rounds other values in their place, can miss the bound.
Values may be sent and summed in bfloat16 or wider, within the bound.
No kernel may reach another device: no remote copies, remote signals or barrier semaphores. Data moves between devices by JAX's collectives and lax.ppermute only.
A program may use at most 128 MiB of HBM per device.

v0:
```python
import math
import jax
import jax.numpy as jnp
from jax import lax
from jax.sharding import PartitionSpec as P

WINDOW = 1024
attn_scale = 168.0 ** (-0.5)
norm_eps = 1e-06


def from_behind(block, axis, distance):
    devices = range(lax.axis_size(axis))
    route = [(i - distance, i) for i in devices if i - distance in devices]
    return lax.ppermute(block, axis, route)


def doc_positions(ids):
    count = ids.shape[0]
    index = jnp.arange(count, dtype=jnp.int32)
    flags = jnp.concatenate([jnp.ones((1,), bool), ids[1:] != ids[:-1]])
    starts = lax.cummax(jnp.where(flags, index, 0), axis=0)
    return index - starts


def norm_rope(inputs, gain, positions):
    values = inputs.astype(jnp.float32)
    meansq = jnp.mean(values * values, axis=-1, keepdims=True)
    scaled = values * lax.rsqrt(meansq + norm_eps) * gain
    width = values.shape[-1]
    half = width // 2
    inverse = 10000.0 ** (-(jnp.arange(half, dtype=jnp.float32) * 2.0 / width))
    angles = positions.astype(jnp.float32)[:, None] * inverse[None, :]
    cosine = jnp.cos(angles)[:, None, :]
    sine = jnp.sin(angles)[:, None, :]
    first = scaled[..., :half]
    second = scaled[..., half:]
    rotated = jnp.concatenate(
        [first * cosine - second * sine, second * cosine + first * sine], axis=-1
    )
    return rotated.astype(jnp.bfloat16)


def on_device(queries_raw, keys_values, doc_ids, q_gain, k_gain, out_weight, post_gain):
    tokens = queries_raw.shape[1]
    head_dim = q_gain.shape[0]
    features = queries_raw.shape[2]
    heads = features // head_dim
    kv_cols = keys_values.shape[2] // 2
    kv_heads = kv_cols // head_dim
    group = heads // kv_heads
    seq_index = lax.axis_index("seq")
    begin = seq_index * tokens
    ids_all = doc_ids[0]
    positions = lax.dynamic_slice_in_dim(doc_positions(ids_all), begin, tokens, 0)
    queries = norm_rope(queries_raw[0].reshape(tokens, heads, head_dim), q_gain, positions)
    queries = queries.reshape(tokens, kv_heads, group, head_dim)
    raw_pairs = keys_values[0]
    keys = norm_rope(raw_pairs[:, :kv_cols].reshape(tokens, kv_heads, head_dim), k_gain, positions)
    local = jnp.concatenate([keys.reshape(tokens, kv_cols), raw_pairs[:, kv_cols:]], axis=1)
    reach = (WINDOW - 2) // tokens + 1
    pieces = []
    for offset in range(reach, 0, -1):
        pieces.append(from_behind(local, "seq", offset))
    pieces.append(local)
    joined = jnp.concatenate(pieces, axis=0)
    span = (reach + 1) * tokens
    ids_pad = jnp.concatenate([jnp.full((reach * tokens,), -1, jnp.int32), ids_all])
    key_ids = lax.dynamic_slice_in_dim(ids_pad, begin, span, 0)
    query_ids = lax.dynamic_slice_in_dim(ids_all, begin, tokens, 0)
    key_rows = joined[:, :kv_cols].reshape(span, kv_heads, head_dim)
    value_rows = joined[:, kv_cols:].reshape(span, kv_heads, head_dim)
    block = math.gcd(tokens, 512)
    relative = (
        reach * tokens
        + jnp.arange(block, dtype=jnp.int32)[:, None]
        - jnp.arange(span, dtype=jnp.int32)[None, :]
    )
    allowed = (relative >= 0) & (relative < WINDOW) & (query_ids[0:block, None] == key_ids[None, :])
    scores = (
        jnp.einsum("tkgd,ukd->kgtu", queries, key_rows, preferred_element_type=jnp.float32)
        * attn_scale
    )
    scores = jnp.where(allowed[None, None], scores, -jnp.inf)
    top = jnp.max(scores, axis=-1, keepdims=True)
    expd = jnp.exp(scores - top)
    total = jnp.sum(expd, axis=-1, keepdims=True)
    probs = (expd / total).astype(jnp.bfloat16)
    mixed = jnp.einsum("kgtu,ukd->tkgd", probs, value_rows, preferred_element_type=jnp.float32)
    outputs = mixed.reshape(block, features).astype(jnp.bfloat16)
    n_fsdp = lax.axis_size("fsdp")
    n_seq = lax.axis_size("seq")
    each = out_weight.shape[0] // n_seq
    mine = lax.dynamic_slice_in_dim(out_weight, begin // tokens * each, each, 0)
    arranged = (
        outputs.reshape(tokens, n_fsdp, n_seq, each).transpose(0, 2, 1, 3).reshape(tokens, features)
    )
    partial_rows = lax.all_gather(mine, "fsdp", axis=0, tiled=True)
    all_rows = lax.all_gather(partial_rows, "seq", axis=0, tiled=True)
    projected = jnp.dot(arranged, all_rows, preferred_element_type=jnp.float32)
    meansq = jnp.mean(projected * projected, axis=-1, keepdims=True)
    result = (projected * lax.rsqrt(meansq + norm_eps) * post_gain).astype(jnp.bfloat16)
    return result[None]


def solution(mesh):
    in_specs = (
        P(("dp", "fsdp"), "seq", None),
        P(("dp", "fsdp"), "seq", None),
        P(("dp", "fsdp"), None),
        P(),
        P(),
        P("fsdp", None),
        P(),
    )
    out_specs = P(("dp", "fsdp"), "seq", None)
    return jax.shard_map(
        on_device, mesh=mesh, in_specs=in_specs, out_specs=out_specs, check_vma=False
    )
```

profile of v0, /device:TPU:64, one launch (start us, length us, event | category | flops | bytes accessed | tf_op | source)
XLA Modules:
  0.0 324.0 jit_solution(14192368447268685597)
XLA Ops:
  6.5 1.8 copy-done
  8.3 0.7 constant_dynamic-slice_fusion
  9.1 56.5 %all-gather.3.cloned.1.call-done = bf16[128,5376]{1,0:T(8,128)(2,1)} async-done(((bf16[16,5376]{1,0:T(8,128)(2,1)}), bf16[128,5376]{1,0:T(8,128)(2,1)}) %all-gather.3.cloned.1.call-update) | async-done | bytes 1376272 | tf_op jit(solution)/shard_map/all_gather | solution.py:98
  65.6 0.9 compare_reduce_fusion
  67.0 1.5 copy.26
  69.7 1.0 pad_maximum_fusion
  70.7 5.7 %collective-permute-start = (bf16[256,2048]{0,1:T(8,128)(2,1)}, bf16[256,2048]{0,1:T(8,128)(2,1)}, u32[]{:S(2)}, u32[]{:S(2)}) collective-permute-start(bf16[256,2048]{0,1:T(8,128)(2,1)} %pad_maximum_fusion), channel_id=1, source_target_pairs={{0,32},{8,40},{16,48},{24,56},{32,64},{40,72},{48,80},{56,88},{64,... | collective-permute-start | bytes 3145736 | tf_op jit(solution)/shard_map/ppermute | solution.py:15
  76.4 1.9 collective-permute-start.1
  78.3 2.6 collective-permute-start.2
  80.9 2.5 collective-permute-start.3
  84.2 0.6 multiply_reduce_fusion.1
  84.9 0.6 add_rsqrt_fusion
  85.5 0.8 copy.28
  86.4 1.4 multiply_multiply_fusion
  87.8 0.8 subtract_convert_fusion
  88.6 1.3 copy.31
  89.9 1.2 copy.32
  91.2 0.5 fusion.8
  91.7 48.3 %collective-permute-done = bf16[256,2048]{0,1:T(8,128)(2,1)} collective-permute-done((bf16[256,2048]{0,1:T(8,128)(2,1)}, bf16[256,2048]{0,1:T(8,128)(2,1)}, u32[]{:S(2)}, u32[]{:S(2)}) %collective-permute-start) | collective-permute-done | bytes 1048608 | tf_op jit(solution)/shard_map/ppermute | solution.py:15
  140.0 1.3 constant_dynamic-update-slice_fusion.4
  141.3 59.7 %collective-permute-done.1 = bf16[256,2048]{0,1:T(8,128)(2,1)} collective-permute-done((bf16[256,2048]{0,1:T(8,128)(2,1)}, bf16[256,2048]{0,1:T(8,128)(2,1)}, u32[]{:S(2)}, u32[]{:S(2)}) %collective-permute-start.1) | collective-permute-done | bytes 1048608 | tf_op jit(solution)/shard_map/ppermute | solution.py:15
  201.0 1.3 constant_dynamic-update-slice_fusion.3
  202.3 43.6 %collective-permute-done.2 = bf16[256,2048]{0,1:T(8,128)(2,1)} collective-permute-done((bf16[256,2048]{0,1:T(8,128)(2,1)}, bf16[256,2048]{0,1:T(8,128)(2,1)}, u32[]{:S(2)}, u32[]{:S(2)}) %collective-permute-start.2) | collective-permute-done | bytes 1048608 | tf_op jit(solution)/shard_map/ppermute | solution.py:15
  245.9 1.3 constant_dynamic-update-slice_fusion.2
  247.2 30.1 %collective-permute-done.3 = bf16[256,2048]{0,1:T(8,128)(2,1)} collective-permute-done((bf16[256,2048]{0,1:T(8,128)(2,1)}, bf16[256,2048]{0,1:T(8,128)(2,1)}, u32[]{:S(2)}, u32[]{:S(2)}) %collective-permute-start.3) | collective-permute-done | bytes 1048608 | tf_op jit(solution)/shard_map/ppermute | solution.py:15
  277.4 1.3 constant_dynamic-update-slice_fusion.1
  278.8 1.8 fusion.19
  280.6 8.7 %exponential_reduce_fusion = f32[8,2,256]{2,1,0:T(2,128)S(1)} fusion(bf16[1280,8,128,1]{0,2,3,1:T(8,128)(2,1)S(1)} %bitcast.63, pred[256,1280]{0,1:T(8,128)(4,1)S(1)} %fusion.8, bf16[256,8,2,64]{3,0,2,1:T(8,128)(2,1)} %bitcast.68, bf16[256,8,2,64]{3,0,2,1:T(8,128)(2,1)} %bitcast.66), kind=kOutput, calls=%fused_computation.4 | convolution fusion | flops 1365247232 | bytes 4014080 | tf_op jit(solution)/shard_map/sub | solution.py:86
  289.3 13.2 %fusion.4 = bf16[8,128,2,256]{3,1,2,0:T(8,128)(2,1)} fusion(bf16[1280,8,128,1]{0,2,3,1:T(8,128)(2,1)} %bitcast.65, f32[8,2,256]{2,1,0:T(2,128)S(1)} %exponential_reduce_fusion, bf16[1280,8,128,1]{0,2,3,1:T(8,128)(2,1)S(1)} %bitcast.64, pred[256,1280]{0,1:T(8,128)(4,1)S(1)} %fusion.8, bf16[256,8,2,64]{3,0,2,1:T(8,128)(2,1)} %bitcast.69, ...), kind=kOutput, calls=%fused_computation.14 | convolution fusion | flops 2713195776 | bytes 7684096 | tf_op jit(solution)/shard_map/kgtu,ukd->tkgd/dot_general | solution.py:89
  302.5 1.3 copy.35
  303.9 10.9 %multiply_reduce_fusion = (f32[256]{0:T(256)S(1)}, f32[256,5376]{1,0:T(8,128)S(1)}) fusion(bf16[256,2048]{0,1:T(8,128)(2,1)S(1)} %bitcast.62, bf16[2048,5376]{1,0:T(8,128)(2,1)} %all-gather.5.cloned.1.call-done), kind=kOutput, calls=%fused_computation.7 | convolution fusion | flops 5639897088 | bytes 28574720 | tf_op jit(solution)/shard_map/dot_general | solution.py:100
  314.9 2.1 fusion.3
  (41 shorter events, 2.9 us)
Async XLA Ops:
  6.5 1.8 copy-start
  6.5 59.1 %all-gather.3.cloned.1.call-start = ((), (), s32[]{:S(2)}) async-start(), calls=%async_computation | async-start | bytes 1548288 | tf_op jit(solution)/shard_map/all_gather | solution.py:98
  9.0 294.8 %all-gather.5.cloned.1.call-start = ((), (), s32[]{:S(2)}) async-start(), calls=%async_computation.1 | async-start | bytes 23396352 | tf_op jit(solution)/shard_map/all_gather | solution.py:99
  65.6 3.7 %copy-start.5 = (f32[128]{0:T(128)S(1)}, f32[128]{0:T(128)}, u32[]{:S(2)}) copy-start(f32[128]{0:T(128)} %param.11) | copy-start | bytes 1540
  69.5 14.1 %copy-start.2 = (bf16[1,256,2048]{2,1,0:T(8,128)(2,1)S(1)}, bf16[1,256,2048]{2,1,0:T(8,128)(2,1)}, u32[]{:S(2)}) copy-start(bf16[1,256,2048]{2,1,0:T(8,128)(2,1)} %param.7) | copy-start | bytes 3145732
  70.7 69.2 %collective-permute-start = (bf16[256,2048]{0,1:T(8,128)(2,1)}, bf16[256,2048]{0,1:T(8,128)(2,1)}, u32[]{:S(2)}, u32[]{:S(2)}) collective-permute-start(bf16[256,2048]{0,1:T(8,128)(2,1)} %pad_maximum_fusion), channel_id=1, source_target_pairs={{0,32},{8,40},{16,48},{24,56},{32,64},{40,72},{48,80},{56,88},{64,... | collective-permute-start | bytes 3145736 | tf_op jit(solution)/shard_map/ppermute | solution.py:15
  76.4 124.6 %collective-permute-start.1 = (bf16[256,2048]{0,1:T(8,128)(2,1)}, bf16[256,2048]{0,1:T(8,128)(2,1)}, u32[]{:S(2)}, u32[]{:S(2)}) collective-permute-start(bf16[256,2048]{0,1:T(8,128)(2,1)} %pad_maximum_fusion), channel_id=1, source_target_pairs={{0,24},{8,32},{16,40},{24,48},{32,56},{40,64},{48,72},{56,80},{64,... | collective-permute-start | bytes 3145736 | tf_op jit(solution)/shard_map/ppermute | solution.py:15
  78.3 167.6 %collective-permute-start.2 = (bf16[256,2048]{0,1:T(8,128)(2,1)}, bf16[256,2048]{0,1:T(8,128)(2,1)}, u32[]{:S(2)}, u32[]{:S(2)}) collective-permute-start(bf16[256,2048]{0,1:T(8,128)(2,1)} %pad_maximum_fusion), channel_id=1, source_target_pairs={{0,16},{8,24},{16,32},{24,40},{32,48},{40,56},{48,64},{56,72},{64,... | collective-permute-start | bytes 3145736 | tf_op jit(solution)/shard_map/ppermute | solution.py:15
  80.9 196.5 %collective-permute-start.3 = (bf16[256,2048]{0,1:T(8,128)(2,1)}, bf16[256,2048]{0,1:T(8,128)(2,1)}, u32[]{:S(2)}, u32[]{:S(2)}) collective-permute-start(bf16[256,2048]{0,1:T(8,128)(2,1)} %pad_maximum_fusion), channel_id=1, source_target_pairs={{0,8},{8,16},{16,24},{24,32},{32,40},{40,48},{48,56},{56,64},{64,7... | collective-permute-start | bytes 3145736 | tf_op jit(solution)/shard_map/ppermute | solution.py:15
  88.6 2.5 copy-start.3
  303.9 11.0 %copy-start.4 = (f32[5376]{0:T(1024)S(1)}, f32[5376]{0:T(1024)}, u32[]{:S(2)}) copy-start(f32[5376]{0:T(1024)} %param.13) | copy-start | bytes 64516
  314.8 2.3 copy-start.1
Sparse Core Ops, SparseCore 0:
  9.9 55.6 all-gather.2
  67.4 225.4 all-gather.4
where the time goes:
time: 325 us; the launch traced here: 324 us
  waiting for transfers between devices  238 us (73%)
  matrix products  32.8 us (10%)
  local copies, waits for them, and re-layouts  16.8 us (5%)
  between operations  13.7 us (4%)
  starting transfers between devices  12.7 us (4%)
  other arithmetic  9.65 us (3%)
    ppermute x4, waiting for transfers between devices, from_behind(): return lax.ppermute(block, axis, route)  182 us
    all_gather x1, waiting for transfers between devices, on_device(): partial_rows = lax.all_gather(mine, 'fsdp', axis=0, tiled=True)  56.5 us
    dot_general x1, matrix products, on_device(): jnp.einsum('kgtu,ukd->tkgd', probs, value_rows, preferred_element_type=jn...  13.2 us
    ppermute x4, starting transfers between devices, from_behind(): return lax.ppermute(block, axis, route)  12.6 us
    dot_general x1, matrix products, on_device(): projected = jnp.dot(arranged, all_rows, preferred_element_type=jnp.float32)  10.9 us
    unnamed x18, local copies, waits for them, and re-layouts  9.05 us
    sub x1, matrix products, on_device(): expd = jnp.exp(scores - top)  8.73 us
  transfers between devices with their start and end apart: 6, of which 5 were waited for; matrix products, arithmetic and copies ran while one was open for 13% of the time, Pallas kernels for 0%

commit v1 on v0

--- a/solution.py
+++ b/solution.py
@@ -95,7 +95,13 @@
     arranged = (
         outputs.reshape(tokens, n_fsdp, n_seq, each).transpose(0, 2, 1, 3).reshape(tokens, features)
     )
-    partial_rows = lax.all_gather(mine, "fsdp", axis=0, tiled=True)
+    tall = jax.lax.all_to_all(
+        jnp.stack([mine] * jax.lax.psum(1, axis_name="fsdp"), axis=0),
+        axis_name="fsdp",
+        split_axis=0,
+        concat_axis=0,
+    )
+    partial_rows = jnp.concatenate(tall, axis=0)
     all_rows = lax.all_gather(partial_rows, "seq", axis=0, tiled=True)
     projected = jnp.dot(arranged, all_rows, preferred_element_type=jnp.float32)
     meansq = jnp.mean(projected * projected, axis=-1, keepdims=True)

time: 325 us -> 293 us (0.902)
  waiting for transfers between devices: 238 us -> 178 us
  blocking collectives: 0 us -> 27.8 us
    all_gather x1 -> x0, waiting for transfers between devices: 56.5 us -> none  [on_device(): partial_rows = lax.all_gather(mine, 'fsdp', axis=0, tiled=True)]
    all_to_all x0 -> x1, blocking collectives: none -> 27.8 us  [on_device(): jax.lax.all_to_all(jnp.stack([mine] * jax.lax.psum(1, axis_name='fsdp'),...]
    ppermute x4, waiting for transfers between devices: 182 us -> 178 us  [from_behind(): return lax.ppermute(block, axis, route)]
    unnamed x18 -> x20, local copies, waits for them, and re-layouts: 9.05 us -> 8.1 us
  transfers between devices with their start and end apart: 6 -> 5, of which waited for: 5 -> 4; matrix products, arithmetic and copies ran while one was open for 13% -> 15% of each run, Pallas kernels for 0% -> 0%
where the time goes in v1:
time: 293 us; the launch traced here: 292 us
  waiting for transfers between devices  178 us (61%)
  matrix products  32.8 us (11%)
  blocking collectives  27.8 us (9%)
  local copies, waits for them, and re-layouts  15.9 us (5%)
  starting transfers between devices  14.4 us (5%)
  between operations  13.7 us (5%)
  other arithmetic  9.56 us (3%)
    ppermute x4, waiting for transfers between devices, from_behind(): return lax.ppermute(block, axis, route)  178 us
    all_to_all x1, blocking collectives, on_device(): jax.lax.all_to_all(jnp.stack([mine] * jax.lax.psum(1, axis_name='fsdp'),...  27.8 us
    ppermute x4, starting transfers between devices, from_behind(): return lax.ppermute(block, axis, route)  14.4 us
    dot_general x1, matrix products, on_device(): jnp.einsum('kgtu,ukd->tkgd', probs, value_rows, preferred_element_type=jn...  13.2 us
    dot_general x1, matrix products, on_device(): projected = jnp.dot(arranged, all_rows, preferred_element_type=jnp.float32)  10.9 us
    sub x1, matrix products, on_device(): expd = jnp.exp(scores - top)  8.73 us
    unnamed x20, local copies, waits for them, and re-layouts  8.1 us
  transfers between devices with their start and end apart: 5, of which 4 were waited for; matrix products, arithmetic and copies ran while one was open for 15% of the time, Pallas kernels for 0%

profile of v1, /device:TPU:64, one launch (start us, length us, event | category | flops | bytes accessed | tf_op | source)
XLA Modules:
  0.0 292.1 jit_solution(6995103683573693512)
XLA Ops:
  6.5 1.8 copy-done
  8.5 27.8 %all_to_all.5 = bf16[8,16,5376]{2,1,0:T(8,128)(2,1)} all-to-all(bf16[8,16,5376]{2,1,0:T(8,128)(2,1)S(1)} %stack.2), channel_id=1, replica_groups=mesh['dp'=2,'seq'=16,'fsdp'=8] {'fsdp'}, dimensions={0} | all-to-all | bytes 2752512 | tf_op jit(solution)/shard_map/all_to_all | solution.py:98
  36.9 0.5 copy.26
  38.6 1.0 pad_maximum_fusion
  39.7 6.4 %collective-permute-start = (bf16[256,2048]{0,1:T(8,128)(2,1)}, bf16[256,2048]{0,1:T(8,128)(2,1)}, u32[]{:S(2)}, u32[]{:S(2)}) collective-permute-start(bf16[256,2048]{0,1:T(8,128)(2,1)} %pad_maximum_fusion), channel_id=1, source_target_pairs={{0,32},{8,40},{16,48},{24,56},{32,64},{40,72},{48,80},{56,88},{64,... | collective-permute-start | bytes 3145736 | tf_op jit(solution)/shard_map/ppermute | solution.py:15
  46.1 1.9 collective-permute-start.1
  48.0 2.9 %collective-permute-start.2 = (bf16[256,2048]{0,1:T(8,128)(2,1)}, bf16[256,2048]{0,1:T(8,128)(2,1)}, u32[]{:S(2)}, u32[]{:S(2)}) collective-permute-start(bf16[256,2048]{0,1:T(8,128)(2,1)} %pad_maximum_fusion), channel_id=1, source_target_pairs={{0,16},{8,24},{16,32},{24,40},{32,48},{40,56},{48,64},{56,72},{64,... | collective-permute-start | bytes 3145736 | tf_op jit(solution)/shard_map/ppermute | solution.py:15
  50.9 3.2 %collective-permute-start.3 = (bf16[256,2048]{0,1:T(8,128)(2,1)}, bf16[256,2048]{0,1:T(8,128)(2,1)}, u32[]{:S(2)}, u32[]{:S(2)}) collective-permute-start(bf16[256,2048]{0,1:T(8,128)(2,1)} %pad_maximum_fusion), channel_id=1, source_target_pairs={{0,8},{8,16},{16,24},{24,32},{32,40},{40,48},{48,56},{56,64},{64,7... | collective-permute-start | bytes 3145736 | tf_op jit(solution)/shard_map/ppermute | solution.py:15
  54.6 0.4 copy.41
  55.0 0.6 multiply_reduce_fusion.1
  55.6 0.7 copy.27
  56.3 1.3 add_rsqrt_fusion
  57.6 0.8 copy.28
  58.4 1.4 multiply_multiply_fusion
  59.9 0.8 subtract_convert_fusion
  60.6 1.3 copy.31
  61.9 1.2 copy.32
  63.2 0.5 fusion.8
  63.7 46.0 %collective-permute-done = bf16[256,2048]{0,1:T(8,128)(2,1)} collective-permute-done((bf16[256,2048]{0,1:T(8,128)(2,1)}, bf16[256,2048]{0,1:T(8,128)(2,1)}, u32[]{:S(2)}, u32[]{:S(2)}) %collective-permute-start) | collective-permute-done | bytes 1048608 | tf_op jit(solution)/shard_map/ppermute | solution.py:15
  109.7 1.3 constant_dynamic-update-slice_fusion.4
  111.0 59.3 %collective-permute-done.1 = bf16[256,2048]{0,1:T(8,128)(2,1)} collective-permute-done((bf16[256,2048]{0,1:T(8,128)(2,1)}, bf16[256,2048]{0,1:T(8,128)(2,1)}, u32[]{:S(2)}, u32[]{:S(2)}) %collective-permute-start.1) | collective-permute-done | bytes 1048608 | tf_op jit(solution)/shard_map/ppermute | solution.py:15
  170.3 1.3 constant_dynamic-update-slice_fusion.3
  171.6 43.6 %collective-permute-done.2 = bf16[256,2048]{0,1:T(8,128)(2,1)} collective-permute-done((bf16[256,2048]{0,1:T(8,128)(2,1)}, bf16[256,2048]{0,1:T(8,128)(2,1)}, u32[]{:S(2)}, u32[]{:S(2)}) %collective-permute-start.2) | collective-permute-done | bytes 1048608 | tf_op jit(solution)/shard_map/ppermute | solution.py:15
  215.2 1.3 constant_dynamic-update-slice_fusion.2
  216.5 29.0 %collective-permute-done.3 = bf16[256,2048]{0,1:T(8,128)(2,1)} collective-permute-done((bf16[256,2048]{0,1:T(8,128)(2,1)}, bf16[256,2048]{0,1:T(8,128)(2,1)}, u32[]{:S(2)}, u32[]{:S(2)}) %collective-permute-start.3) | collective-permute-done | bytes 1048608 | tf_op jit(solution)/shard_map/ppermute | solution.py:15
  245.5 1.3 constant_dynamic-update-slice_fusion.1
  246.9 1.8 fusion.19
  248.7 8.7 %exponential_reduce_fusion = f32[8,2,256]{2,1,0:T(2,128)S(1)} fusion(bf16[1280,8,128,1]{0,2,3,1:T(8,128)(2,1)S(1)} %bitcast.65, pred[256,1280]{0,1:T(8,128)(4,1)S(1)} %fusion.8, bf16[256,8,2,64]{3,0,2,1:T(8,128)(2,1)} %bitcast.70, bf16[256,8,2,64]{3,0,2,1:T(8,128)(2,1)} %bitcast.68), kind=kOutput, calls=%fused_computation.4 | convolution fusion | flops 1365247232 | bytes 4014080 | tf_op jit(solution)/shard_map/sub | solution.py:86
  257.5 13.2 %fusion.4 = bf16[8,128,2,256]{3,1,2,0:T(8,128)(2,1)} fusion(bf16[1280,8,128,1]{0,2,3,1:T(8,128)(2,1)} %bitcast.67, f32[8,2,256]{2,1,0:T(2,128)S(1)} %exponential_reduce_fusion, bf16[1280,8,128,1]{0,2,3,1:T(8,128)(2,1)S(1)} %bitcast.66, pred[256,1280]{0,1:T(8,128)(4,1)S(1)} %fusion.8, bf16[256,8,2,64]{3,0,2,1:T(8,128)(2,1)} %bitcast.71, ...), kind=kOutput, calls=%fused_computation.14 | convolution fusion | flops 2713195776 | bytes 7684096 | tf_op jit(solution)/shard_map/kgtu,ukd->tkgd/dot_general | solution.py:89
  270.6 1.3 copy.35
  272.0 10.9 %multiply_reduce_fusion = (f32[256]{0:T(256)S(1)}, f32[256,5376]{1,0:T(8,128)S(1)}) fusion(bf16[256,2048]{0,1:T(8,128)(2,1)S(1)} %bitcast.64, bf16[2048,5376]{1,0:T(8,128)(2,1)} %all-gather.2.cloned.1.call-done), kind=kOutput, calls=%fused_computation.7 | convolution fusion | flops 5639897088 | bytes 28574720 | tf_op jit(solution)/shard_map/dot_general | solution.py:106
  283.0 2.1 fusion.3
  (42 shorter events, 2.7 us)
Async XLA Ops:
  6.5 1.8 copy-start
  6.5 265.4 %all-gather.2.cloned.1.call-start = ((), (), s32[]{:S(2)}) async-start(), calls=%async_computation.1 | async-start | bytes 23396352 | tf_op jit(solution)/shard_map/all_gather | solution.py:105
  8.3 27.9 %copy-start.4 = (s32[1,4096]{1,0:T(1,128)S(1)}, s32[1,4096]{1,0:T(1,128)}, u32[]{:S(2)}) copy-start(s32[1,4096]{1,0:T(1,128)} %param.9) | copy-start | bytes 49156
  8.3 28.6 %copy-start.3 = (bf16[1,256,2048]{2,1,0:T(8,128)(2,1)S(1)}, bf16[1,256,2048]{2,1,0:T(8,128)(2,1)}, u32[]{:S(2)}) copy-start(bf16[1,256,2048]{2,1,0:T(8,128)(2,1)} %param.8) | copy-start | bytes 3145732
  36.2 2.0 copy-start.6
  38.4 15.9 %copy-start.2 = (bf16[1,256,2048]{2,1,0:T(8,128)(2,1)S(1)}, bf16[1,256,2048]{2,1,0:T(8,128)(2,1)}, u32[]{:S(2)}) copy-start(bf16[1,256,2048]{2,1,0:T(8,128)(2,1)} %param.7) | copy-start | bytes 3145732
  39.7 70.0 %collective-permute-start = (bf16[256,2048]{0,1:T(8,128)(2,1)}, bf16[256,2048]{0,1:T(8,128)(2,1)}, u32[]{:S(2)}, u32[]{:S(2)}) collective-permute-start(bf16[256,2048]{0,1:T(8,128)(2,1)} %pad_maximum_fusion), channel_id=1, source_target_pairs={{0,32},{8,40},{16,48},{24,56},{32,64},{40,72},{48,80},{56,88},{64,... | collective-permute-start | bytes 3145736 | tf_op jit(solution)/shard_map/ppermute | solution.py:15
  46.1 124.2 %collective-permute-start.1 = (bf16[256,2048]{0,1:T(8,128)(2,1)}, bf16[256,2048]{0,1:T(8,128)(2,1)}, u32[]{:S(2)}, u32[]{:S(2)}) collective-permute-start(bf16[256,2048]{0,1:T(8,128)(2,1)} %pad_maximum_fusion), channel_id=1, source_target_pairs={{0,24},{8,32},{16,40},{24,48},{32,56},{40,64},{48,72},{56,80},{64,... | collective-permute-start | bytes 3145736 | tf_op jit(solution)/shard_map/ppermute | solution.py:15
  48.0 167.3 %collective-permute-start.2 = (bf16[256,2048]{0,1:T(8,128)(2,1)}, bf16[256,2048]{0,1:T(8,128)(2,1)}, u32[]{:S(2)}, u32[]{:S(2)}) collective-permute-start(bf16[256,2048]{0,1:T(8,128)(2,1)} %pad_maximum_fusion), channel_id=1, source_target_pairs={{0,16},{8,24},{16,32},{24,40},{32,48},{40,56},{48,64},{56,72},{64,... | collective-permute-start | bytes 3145736 | tf_op jit(solution)/shard_map/ppermute | solution.py:15
  50.9 194.6 %collective-permute-start.3 = (bf16[256,2048]{0,1:T(8,128)(2,1)}, bf16[256,2048]{0,1:T(8,128)(2,1)}, u32[]{:S(2)}, u32[]{:S(2)}) collective-permute-start(bf16[256,2048]{0,1:T(8,128)(2,1)} %pad_maximum_fusion), channel_id=1, source_target_pairs={{0,8},{8,16},{16,24},{24,32},{32,40},{40,48},{48,56},{56,64},{64,7... | collective-permute-start | bytes 3145736 | tf_op jit(solution)/shard_map/ppermute | solution.py:15
  272.0 11.0 %copy-start.5 = (f32[5376]{0:T(1024)S(1)}, f32[5376]{0:T(1024)}, u32[]{:S(2)}) copy-start(f32[5376]{0:T(1024)} %param.13) | copy-start | bytes 64516
  283.0 2.3 copy-start.1
Sparse Core Ops, SparseCore 0:
  36.4 224.5 all-gather.1
